TPU v7x, 32 devices: a whole 2x2x4 slice. The times are simulated.
32 devices in a mesh: tm: 4 (over z), space: 8 (over y, x, core).
Axes of the slice: x: 2, y: 2, z: 4, core: 2. Of those that a mesh axis runs over, the one named last changes fastest.
Arguments:
- queries: bfloat16 [4096, 2560], P(('tm', 'space')), may hold values from -6 to 6
- keys: bfloat16 [4096, 2560], P(('tm', 'space')), may hold values from -6 to 6
- values: bfloat16 [4096, 2560], P(('tm', 'space')), may hold values from -6 to 6
- grad_out: bfloat16 [4096, 2560], P(('tm', 'space')), may hold values from -6 to 6
- saved_state: bfloat16 [4, 20, 128, 128], P('tm', None, 'space'), may hold values from -0.3984375 to 0.3984375
Outputs:
- grad_q: bfloat16 [4096, 2560], P(('tm', 'space'))
- grad_k: bfloat16 [4096, 2560], P(('tm', 'space'))
- grad_v: bfloat16 [4096, 2560], P(('tm', 'space'))
All inputs are finite; a program needn't handle non-finite values.
Results may differ from a plain program's by a relative error of at most 0.0049.
Values may be sent and summed in bfloat16 or wider, within the bound.
No kernel may reach another device: no remote copies, remote signals or barrier semaphores. Data moves between devices by JAX's collectives and lax.ppermute only.
A program may use at most 64 MiB of HBM per device.

v0:
```python
import functools
import math

import jax
import jax.numpy as jnp
from jax import lax
from jax.experimental import pallas as pl
from jax.experimental.pallas import tpu as pltpu
from jax.sharding import PartitionSpec as P

CONTRACT_ROWS = (((0,), (0,)), ((), ()))
CONTRACT_COLS = (((1,), (1,)), ((), ()))
VMEM_BYTES = 16 * 1024 * 1024
ANYWHERE = pl.BlockSpec(memory_space=pl.ANY)
IN_VMEM = pl.BlockSpec(memory_space=pltpu.VMEM)


def power_of_two(count):
    return count & (count - 1) == 0


def partner(group, hop, groups):
    if power_of_two(groups):
        return group ^ hop
    return (group + hop) % groups


def source(group, hop, groups):
    if power_of_two(groups):
        return group ^ hop
    return (group - hop + groups) % groups


def cost(flops, *arrays):
    moved = sum(array.size * array.dtype.itemsize for array in arrays)
    return pl.CostEstimate(flops=flops, bytes_accessed=moved, transcendentals=0)


def after(value, earlier):
    return lax.optimization_barrier((value, earlier))[0]


def place_on_space(lanes):
    index = lax.axis_index("space")
    return lax.div(index, lanes), lax.rem(index, lanes)


def swap_lanes(value, lanes, groups):
    pairs = [(g * lanes + c, g * lanes + 1 - c) for g in range(groups) for c in range(lanes)]
    return lax.ppermute(value, "space", pairs)


def hop_groups(value, hop, lanes, groups):
    pairs = [
        (g * lanes + c, partner(g, hop, groups) * lanes + c)
        for g in range(groups)
        for c in range(lanes)
    ]
    return lax.ppermute(value, "space", pairs)


def gather_groups(value, waits, lanes, groups):
    if power_of_two(groups):
        for step in range(groups.bit_length() - 1):
            start, done = waits[min(step, len(waits) - 1)]
            met = hop_groups(after(value, start), 1 << step, lanes, groups)
            value = jnp.concatenate([value, after(met, done)])
        return value
    return jnp.concatenate(
        [value] + [hop_groups(value, hop, lanes, groups) for hop in range(1, groups)]
    )


def products(scale, queries, grad_out):
    return scale * lax.dot_general(
        jnp.maximum(queries, 0),
        grad_out,
        CONTRACT_ROWS,
        preferred_element_type=jnp.float32,
    )


def partial_kernel(lanes, other, scale, q_ref, o_ref, part_ref):
    span, head = part_ref.shape
    _, lane = place_on_space(lanes)
    base = (1 - lane if other else lane) * span
    for h in range(span // head):
        rows = pl.ds(h * head, head)
        cols = pl.ds(pl.multiple_of(base + h * head, head), head)
        part_ref[rows, :] = products(
            scale, q_ref[:, rows if other else cols], o_ref[:, cols]
        ).astype(part_ref.dtype)


def partial_products(queries, grad_out, head, lanes, other, scale):
    tokens, width = grad_out.shape
    span = width // lanes
    return pl.pallas_call(
        functools.partial(partial_kernel, lanes, other, scale),
        out_shape=jax.ShapeDtypeStruct((span, head), jnp.bfloat16 if other else jnp.float32),
        in_specs=[IN_VMEM, IN_VMEM],
        out_specs=IN_VMEM,
        compiler_params=pltpu.CompilerParams(vmem_limit_bytes=VMEM_BYTES),
        cost_estimate=cost(2 * tokens * span * head, queries),
        name="partial_other" if other else "partial_own",
    )(queries, grad_out)


def cut_kernel(lanes, groups, *refs):
    parts, outs = refs[:lanes], refs[lanes:]
    group, _ = place_on_space(lanes)
    rows = outs[0].shape[0]
    for hop, out_ref in enumerate(outs):
        there = pl.ds(pl.multiple_of(partner(group, hop, groups) * rows, rows), rows)
        total = parts[0][there, :]
        for part in parts[1:]:
            total = total + part[there, :].astype(jnp.float32)
        out_ref[...] = total.astype(out_ref.dtype)


def cut_by_group(parts, lanes, groups):
    span, head = parts[0].shape
    rows = span // groups
    outs = [jax.ShapeDtypeStruct((rows, head), jnp.float32)]
    outs += [jax.ShapeDtypeStruct((rows, head), jnp.bfloat16)] * (groups - 1)
    return pl.pallas_call(
        functools.partial(cut_kernel, lanes, groups),
        out_shape=outs,
        in_specs=[IN_VMEM] * lanes,
        out_specs=[IN_VMEM] * groups,
        compiler_params=pltpu.CompilerParams(vmem_limit_bytes=VMEM_BYTES),
        cost_estimate=cost(span * head, *parts),
        name="cut_by_group",
    )(*parts)


def key_value_products(k_ref, v_ref, state, cols, dk_ref, dv_ref):
    head = state.shape[1]
    for h in range(state.shape[0] // head):
        local = pl.ds(h * head, head)
        keys, grad_state = k_ref[:, cols(h)], state[local, :]
        full = lax.dot_general(
            v_ref[:, cols(h)], grad_state, CONTRACT_COLS, preferred_element_type=jnp.float32
        )
        dk_ref[:, local] = jnp.where(keys > 0, full, 0.0).astype(dk_ref.dtype)
        dv_ref[:, local] = jnp.dot(
            jnp.maximum(keys, 0), grad_state, preferred_element_type=jnp.float32
        ).astype(dv_ref.dtype)
        yield h


def place_pieces(pieces, group, groups, state):
    for hop, piece in enumerate(pieces):
        rows = piece.shape[0]
        owner = source(group, hop, groups)
        state[pl.ds(pl.multiple_of(owner * rows, rows), rows), :] = piece[...]


def near_kernel(lanes, groups, q_ref, o_ref, k_ref, v_ref, *rest):
    sides, pieces = rest[:lanes], rest[lanes : lanes + groups]
    dq_ref, dk_ref, dv_ref, saved, state, sems = rest[lanes + groups :]
    heads, head, _ = saved.shape
    rows = sides[0].shape[2]
    group, lane = place_on_space(lanes)
    copies = []
    for other, side in enumerate(sides):
        there = 1 - lane if other else lane
        for hop in range(groups):
            owner = source(group, hop, groups) * lanes + there
            dst = pl.ds(pl.multiple_of(owner * rows, rows), rows)
            if rows % 16 == 0:
                saved[:, dst, :] = side[hop]
            else:
                copies.append(
                    pltpu.make_async_copy(side.at[hop], saved.at[:, dst, :], sems.at[other, hop])
                )
    for copy in copies:
        copy.start()
    for copy in copies:
        copy.wait()
    for h in range(heads):
        cols = pl.ds(h * head, head)
        full = lax.dot_general(
            o_ref[:, cols], saved[h], CONTRACT_COLS, preferred_element_type=jnp.float32
        )
        dq_ref[:, cols] = jnp.where(q_ref[:, cols] > 0, full, 0.0).astype(dq_ref.dtype)
    place_pieces(pieces, group, groups, state)
    base = lane * state.shape[0]
    for _ in key_value_products(
        k_ref,
        v_ref,
        state,
        lambda h: pl.ds(pl.multiple_of(base + h * head, head), head),
        dk_ref,
        dv_ref,
    ):
        pass


def near_grads(queries, grad_out, keys, values, sides, pieces):
    lanes, groups = len(sides), len(pieces)
    tokens, heads, (rows, head) = queries.shape[0], sides[0].shape[1], pieces[0].shape
    span = groups * rows
    return pl.pallas_call(
        functools.partial(near_kernel, lanes, groups),
        out_shape=(
            jax.ShapeDtypeStruct(queries.shape, queries.dtype),
            jax.ShapeDtypeStruct((tokens, span), keys.dtype),
            jax.ShapeDtypeStruct((tokens, span), values.dtype),
        ),
        in_specs=[IN_VMEM] * (4 + lanes + groups),
        out_specs=(IN_VMEM, IN_VMEM, IN_VMEM),
        scratch_shapes=[
            pltpu.VMEM((heads, head, head), sides[0].dtype),
            pltpu.VMEM((span, head), pieces[0].dtype),
            pltpu.SemaphoreType.DMA((lanes, groups)),
        ],
        compiler_params=pltpu.CompilerParams(vmem_limit_bytes=VMEM_BYTES),
        cost_estimate=cost(4 * queries.size * head, queries, queries, grad_out, *sides),
        name="near_grads",
    )(queries, grad_out, keys, values, *sides, *pieces)


def far_kernel(lanes, groups, k_ref, v_ref, *rest):
    dq_ref, near, pieces = rest[0], rest[1:3], rest[3:-8]
    dq_hbm, *outs = rest[-8:-5]
    state, dk_buf, dv_buf, sems, dq_sem = rest[-5:]
    span, head = state.shape
    group, lane = place_on_space(lanes)
    copies = [pltpu.make_async_copy(dq_ref, dq_hbm, dq_sem)]
    copies[0].start()
    for at in range(2):
        mine = pl.ds(pl.multiple_of(lane * span, head), span)
        copies.append(pltpu.make_async_copy(near[at], outs[at].at[:, mine], sems.at[at, 0]))
        copies[-1].start()
    if pieces:
        place_pieces(pieces, group, groups, state)
        base = (1 - lane) * span
        part = span // head // (sems.shape[1] - 1)
        for h in key_value_products(
            k_ref,
            v_ref,
            state,
            lambda h: pl.ds(pl.multiple_of(base + h * head, head), head),
            dk_buf,
            dv_buf,
        ):
            if (h + 1) % part == 0:
                src = pl.ds((h + 1 - part) * head, part * head)
                dst = pl.ds(pl.multiple_of(base + (h + 1 - part) * head, head), part * head)
                for at, buf in enumerate((dk_buf, dv_buf)):
                    copies.append(
                        pltpu.make_async_copy(
                            buf.at[:, src], outs[at].at[:, dst], sems.at[at, 1 + h // part]
                        )
                    )
                    copies[-1].start()
    for copy in copies:
        copy.wait()


def far_grads(keys, values, near, pieces, lanes, groups):
    tokens, span = near[1].shape
    head = pieces[0].shape[1] if pieces else span
    return pl.pallas_call(
        functools.partial(far_kernel, lanes, groups),
        out_shape=(
            jax.ShapeDtypeStruct(near[0].shape, near[0].dtype),
            jax.ShapeDtypeStruct(keys.shape, keys.dtype),
            jax.ShapeDtypeStruct(values.shape, values.dtype),
        ),
        in_specs=[IN_VMEM] * (5 + len(pieces)),
        out_specs=(ANYWHERE,) * 3,
        scratch_shapes=[
            pltpu.VMEM((span, head), keys.dtype),
            pltpu.VMEM((tokens, span), keys.dtype),
            pltpu.VMEM((tokens, span), values.dtype),
            pltpu.SemaphoreType.DMA((2, 1 + math.gcd(span // head, 5))),
            pltpu.SemaphoreType.DMA,
        ],
        compiler_params=pltpu.CompilerParams(vmem_limit_bytes=VMEM_BYTES),
        cost_estimate=cost(4 * tokens * span * head, *near),
        name="far_grads",
    )(keys, values, *near, *pieces)


def suffix_sum(share, blocks):
    block = lax.axis_index("tm")
    suffix = total = first = share
    if power_of_two(blocks):
        hop = 1
        while hop < blocks:
            pairs = [(b, b ^ hop) for b in range(blocks)]
            met = lax.ppermute(total.astype(jnp.bfloat16), "tm", pairs).astype(jnp.float32)
            suffix = suffix + jnp.where(block & hop == 0, met, 0.0)
            total = total + met
            first = total if hop == 1 else first
            hop *= 2
    else:
        for hop in range(1, blocks):
            pairs = [(b, b - hop) for b in range(hop, blocks)]
            later = lax.ppermute(share.astype(jnp.bfloat16), "tm", pairs)
            suffix = suffix + later.astype(jnp.float32)
    return suffix.astype(jnp.bfloat16), first


def per_device(queries, keys, values, grad_out, saved_state):
    heads, _, head = saved_state.shape[1:]
    blocks, devices = lax.axis_size("tm"), lax.axis_size("space")
    lanes = 2 if devices % 2 == 0 and heads % 2 == 0 else 1
    groups = devices // lanes
    far_first = range(groups - 1, 0, -1)
    scale = 1.0 / math.sqrt(queries.shape[0] * blocks * devices * head)

    parts = []
    if lanes > 1:
        _, lane = place_on_space(lanes)
        span = queries.shape[1] // lanes
        starts = (jnp.zeros_like(lane), (1 - lane) * span)
        cut = lax.dynamic_slice(
            queries, starts, (queries.shape[0], span), allow_negative_indices=False
        )
        theirs = partial_products(cut, grad_out, head, lanes, True, scale)
        parts.append(swap_lanes(theirs, lanes, groups))
        queries = after(queries, cut)
    parts.insert(0, partial_products(queries, grad_out, head, lanes, False, scale))
    share, *sends = cut_by_group(parts, lanes, groups)
    for hop in far_first:
        share = share + hop_groups(sends[hop - 1], hop, lanes, groups).astype(jnp.float32)
    own, first = suffix_sum(share, blocks)
    met = [hop_groups(own, hop, lanes, groups) for hop in far_first]

    saved = gather_groups(saved_state, [(parts[0], ()), (share, ())], lanes, groups)
    sides = [saved] + ([swap_lanes(saved, lanes, groups)] if lanes > 1 else [])

    near = [own, *met[::-1]]
    far = [swap_lanes(piece, lanes, groups) for piece in near] if lanes > 1 else []
    ready = near_grads(queries, grad_out, keys, values, sides, near)
    return far_grads(keys, values, ready, far, lanes, groups)


def solution(mesh):
    tokens = P(("tm", "space"), None)
    return jax.shard_map(
        per_device,
        mesh=mesh,
        in_specs=(tokens, tokens, tokens, tokens, P("tm", None, "space", None)),
        out_specs=(tokens, tokens, tokens),
        check_vma=False,
    )
```

profile of v0, /device:TPU:0, one launch (start us, length us, event | category | flops | bytes accessed | tf_op | source)
XLA Modules:
  0.0 33.0 jit_solution(12163312082015194590)
XLA Ops:
  0.6 1.1 %constant_dynamic-slice_fusion.q_ref = bf16[128,1280]{1,0:T(8,128)(2,1)S(1)} fusion(bf16[128,2560]{1,0:T(8,128)(2,1)} %q_ref.1, s32[]{:T(128)S(6)} %mul.3), kind=kLoop, calls=%fused_computation.9 | loop fusion | bytes 655364 | tf_op jit(solution)/shard_map/dynamic_slice | solution.py:320
  1.7 0.1 copy-done
  1.8 0.3 partial_other.1
  2.1 0.0 copy-start.4
  2.1 0.5 %collective-permute-start.1 = (bf16[1280,128]{1,0:T(8,128)(2,1)S(1)}, bf16[1280,128]{1,0:T(8,128)(2,1)S(1)}, u32[]{:S(2)}, u32[]{:S(2)}) collective-permute-start(bf16[1280,128]{1,0:T(8,128)(2,1)S(1)} %partial_other.1), channel_id=1, source_target_pairs={{0,1},{1,0},{2,3},{3,2},{4,5},{5,4},{6,7},{7,6},{8,9},{9,8},{10,11... | collective-permute-start | bytes 983048 | tf_op jit(solution)/shard_map/ppermute | solution.py:50
  2.6 0.3 copy-done.1
  2.9 0.3 partial_own.1.refs_0_
  3.2 3.0 %collective-permute-start = (bf16[1,20,16,128]{3,2,1,0:T(8,128)(2,1)S(1)}, bf16[1,20,16,128]{3,2,1,0:T(8,128)(2,1)S(1)}, u32[]{:S(2)}, u32[]{:S(2)}) collective-permute-start(bf16[1,20,16,128]{3,2,1,0:T(8,128)(2,1)S(1)} %copy-done.4), channel_id=1, source_target_pairs={{0,2},{1,3},{2,0},{3,1},{4,6},{5,7},{6,4},{7,5},{8,10},{9,11},{10,... | collective-permute-start | bytes 245768 | tf_op jit(solution)/shard_map/ppermute | solution.py:59
  6.2 0.1 cut_by_group.1
  6.3 1.6 %collective-permute-start.2 = (bf16[320,128]{1,0:T(8,128)(2,1)S(1)}, bf16[320,128]{1,0:T(8,128)(2,1)S(1)}, u32[]{:S(2)}, u32[]{:S(2)}) collective-permute-start(bf16[320,128]{1,0:T(8,128)(2,1)S(1)} %get-tuple-element.16), channel_id=1, source_target_pairs={{0,6},{1,7},{2,4},{3,5},{4,2},{5,3},{6,0},{7,1},{8,14},{9,15},{10,... | collective-permute-start | bytes 245768 | tf_op jit(solution)/shard_map/ppermute | solution.py:59
  7.8 0.5 %collective-permute-start.3 = (bf16[320,128]{1,0:T(8,128)(2,1)S(1)}, bf16[320,128]{1,0:T(8,128)(2,1)S(1)}, u32[]{:S(2)}, u32[]{:S(2)}) collective-permute-start(bf16[320,128]{1,0:T(8,128)(2,1)S(1)} %get-tuple-element.17), channel_id=1, source_target_pairs={{0,4},{1,5},{2,6},{3,7},{4,0},{5,1},{6,2},{7,3},{8,12},{9,13},{10,... | collective-permute-start | bytes 245768 | tf_op jit(solution)/shard_map/ppermute | solution.py:59
  8.3 1.5 %collective-permute-start.4 = (bf16[320,128]{1,0:T(8,128)(2,1)S(1)}, bf16[320,128]{1,0:T(8,128)(2,1)S(1)}, u32[]{:S(2)}, u32[]{:S(2)}) collective-permute-start(bf16[320,128]{1,0:T(8,128)(2,1)S(1)} %get-tuple-element.18), channel_id=1, source_target_pairs={{0,2},{1,3},{2,0},{3,1},{4,6},{5,7},{6,4},{7,5},{8,10},{9,11},{10,... | collective-permute-start | bytes 245768 | tf_op jit(solution)/shard_map/ppermute | solution.py:59
  9.8 2.4 %collective-permute-done.2 = bf16[320,128]{1,0:T(8,128)(2,1)S(1)} collective-permute-done((bf16[320,128]{1,0:T(8,128)(2,1)S(1)}, bf16[320,128]{1,0:T(8,128)(2,1)S(1)}, u32[]{:S(2)}, u32[]{:S(2)}) %collective-permute-start.2) | collective-permute-done | bytes 81952 | tf_op jit(solution)/shard_map/ppermute | solution.py:59
  12.2 1.2 %collective-permute-done.3 = bf16[320,128]{1,0:T(8,128)(2,1)S(1)} collective-permute-done((bf16[320,128]{1,0:T(8,128)(2,1)S(1)}, bf16[320,128]{1,0:T(8,128)(2,1)S(1)}, u32[]{:S(2)}, u32[]{:S(2)}) %collective-permute-start.3) | collective-permute-done | bytes 81952 | tf_op jit(solution)/shard_map/ppermute | solution.py:59
  13.4 1.6 %collective-permute-start.7 = (bf16[320,128]{1,0:T(8,128)(2,1)S(1)}, bf16[320,128]{1,0:T(8,128)(2,1)S(1)}, u32[]{:S(2)}, u32[]{:S(2)}) collective-permute-start(bf16[320,128]{1,0:T(8,128)(2,1)S(1)} %get-tuple-element.23), channel_id=1, source_target_pairs={{0,8},{8,0},{16,24},{24,16},{1,9},{9,1},{17,25},{25,17},{2,10},{10... | collective-permute-start | bytes 245768 | tf_op jit(solution)/shard_map/ppermute | solution.py:294
  15.1 0.0 copy-start.2
  15.1 1.0 %collective-permute-start.5 = (bf16[2,20,16,128]{3,2,1,0:T(8,128)(2,1)S(1)}, bf16[2,20,16,128]{3,2,1,0:T(8,128)(2,1)S(1)}, u32[]{:S(2)}, u32[]{:S(2)}) collective-permute-start(bf16[2,20,16,128]{3,2,1,0:T(8,128)(2,1)S(1)} %pad_maximum_fusion.1), channel_id=1, source_target_pairs={{0,4},{1,5},{2,6},{3,7},{4,0},{5,1},{6,2},{7,3},{8,12},{9,13},{10,... | collective-permute-start | bytes 491528 | tf_op jit(solution)/shard_map/ppermute | solution.py:59
  16.1 1.8 %collective-permute-done.7 = bf16[320,128]{1,0:T(8,128)(2,1)S(1)} collective-permute-done((bf16[320,128]{1,0:T(8,128)(2,1)S(1)}, bf16[320,128]{1,0:T(8,128)(2,1)S(1)}, u32[]{:S(2)}, u32[]{:S(2)}) %collective-permute-start.7) | collective-permute-done | bytes 81952 | tf_op jit(solution)/shard_map/ppermute | solution.py:294
  17.9 2.7 %collective-permute-start.8 = (bf16[320,128]{1,0:T(8,128)(2,1)S(1)}, bf16[320,128]{1,0:T(8,128)(2,1)S(1)}, u32[]{:S(2)}, u32[]{:S(2)}) collective-permute-start(bf16[320,128]{1,0:T(8,128)(2,1)S(1)} %fusion.3), channel_id=1, source_target_pairs={{0,16},{8,24},{16,0},{24,8},{1,17},{9,25},{17,1},{25,9},{2,18},{10... | collective-permute-start | bytes 245768 | tf_op jit(solution)/shard_map/ppermute | solution.py:294
  20.6 0.1 collective-permute-done.5
  20.7 0.1 collective-permute-start.6
  20.8 2.5 %collective-permute-done.8 = bf16[320,128]{1,0:T(8,128)(2,1)S(1)} collective-permute-done((bf16[320,128]{1,0:T(8,128)(2,1)S(1)}, bf16[320,128]{1,0:T(8,128)(2,1)S(1)}, u32[]{:S(2)}, u32[]{:S(2)}) %collective-permute-start.8) | collective-permute-done | bytes 81952 | tf_op jit(solution)/shard_map/ppermute | solution.py:294
  23.4 1.9 %collective-permute-start.11 = (bf16[320,128]{1,0:T(8,128)(2,1)S(1)}, bf16[320,128]{1,0:T(8,128)(2,1)S(1)}, u32[]{:S(2)}, u32[]{:S(2)}) collective-permute-start(bf16[320,128]{1,0:T(8,128)(2,1)S(1)} %fusion.2.rest_2_), channel_id=1, source_target_pairs={{0,6},{1,7},{2,4},{3,5},{4,2},{5,3},{6,0},{7,1},{8,14},{9,15},{10,... | collective-permute-start | bytes 245768 | tf_op jit(solution)/shard_map/ppermute | solution.py:59
  25.3 0.5 %collective-permute-start.10 = (bf16[320,128]{1,0:T(8,128)(2,1)S(1)}, bf16[320,128]{1,0:T(8,128)(2,1)S(1)}, u32[]{:S(2)}, u32[]{:S(2)}) collective-permute-start(bf16[320,128]{1,0:T(8,128)(2,1)S(1)} %fusion.2.rest_2_), channel_id=1, source_target_pairs={{0,4},{1,5},{2,6},{3,7},{4,0},{5,1},{6,2},{7,3},{8,12},{9,13},{10,... | collective-permute-start | bytes 245768 | tf_op jit(solution)/shard_map/ppermute | solution.py:59
  25.8 1.1 %collective-permute-start.9 = (bf16[320,128]{1,0:T(8,128)(2,1)S(1)}, bf16[320,128]{1,0:T(8,128)(2,1)S(1)}, u32[]{:S(2)}, u32[]{:S(2)}) collective-permute-start(bf16[320,128]{1,0:T(8,128)(2,1)S(1)} %fusion.2.rest_2_), channel_id=1, source_target_pairs={{0,2},{1,3},{2,0},{3,1},{4,6},{5,7},{6,4},{7,5},{8,10},{9,11},{10,... | collective-permute-start | bytes 245768 | tf_op jit(solution)/shard_map/ppermute | solution.py:59
  26.9 1.8 %collective-permute-done.11.rest_5_ = bf16[320,128]{1,0:T(8,128)(2,1)S(1)} collective-permute-done((bf16[320,128]{1,0:T(8,128)(2,1)S(1)}, bf16[320,128]{1,0:T(8,128)(2,1)S(1)}, u32[]{:S(2)}, u32[]{:S(2)}) %collective-permute-start.11) | collective-permute-done | bytes 81952 | tf_op jit(solution)/shard_map/ppermute | solution.py:59
  28.8 1.0 %collective-permute-done.10.rest_4_ = bf16[320,128]{1,0:T(8,128)(2,1)S(1)} collective-permute-done((bf16[320,128]{1,0:T(8,128)(2,1)S(1)}, bf16[320,128]{1,0:T(8,128)(2,1)S(1)}, u32[]{:S(2)}, u32[]{:S(2)}) %collective-permute-start.10) | collective-permute-done | bytes 81952 | tf_op jit(solution)/shard_map/ppermute | solution.py:59
  29.8 0.5 %collective-permute-done.9.rest_3_ = bf16[320,128]{1,0:T(8,128)(2,1)S(1)} collective-permute-done((bf16[320,128]{1,0:T(8,128)(2,1)S(1)}, bf16[320,128]{1,0:T(8,128)(2,1)S(1)}, u32[]{:S(2)}, u32[]{:S(2)}) %collective-permute-start.9) | collective-permute-done | bytes 81952 | tf_op jit(solution)/shard_map/ppermute | solution.py:59
  30.3 0.0 collective-permute-start.13
  30.3 1.0 %near_grads.1 = (bf16[128,2560]{1,0:T(8,128)(2,1)S(1)}, bf16[128,1280]{1,0:T(8,128)(2,1)S(1)}, bf16[128,1280]{1,0:T(8,128)(2,1)S(1)}) custom-call(bf16[128,2560]{1,0:T(8,128)(2,1)S(1)} %copy-done.1, bf16[128,2560]{1,0:T(8,128)(2,1)S(1)} %copy-done, bf16[128,2560]{1,0:T(8,128)(2,1)S(1)} %copy-done.2, bf16[128,2560]{1,0:T(8,128)(2,1)S(1)} %copy-done.3, ...), custom_call_target="tpu_custom_call" | custom-call | flops 167772160 | bytes 2621440 | tf_op jit(solution)/shard_map/near_grads/pallas_call | solution.py:204
  31.3 0.2 collective-permute-done.13.rest_4_
  31.5 1.5 %far_grads.1 = (bf16[128,2560]{1,0:T(8,128)(2,1)}, bf16[128,2560]{1,0:T(8,128)(2,1)}, bf16[128,2560]{1,0:T(8,128)(2,1)}) custom-call(bf16[128,2560]{1,0:T(8,128)(2,1)S(1)} %copy-done.2, bf16[128,2560]{1,0:T(8,128)(2,1)S(1)} %copy-done.3, bf16[128,2560]{1,0:T(8,128)(2,1)S(1)} %get-tuple-element.20.rest_0_, bf16[128,1280]{1,0:T(8,128)(2,1)S(1)} %get-tuple-element.21.rest_1_, ...), custom_call_target="tpu_custom_call" | custom-call | flops 83886080 | bytes 1310720 | tf_op jit(solution)/shard_map/far_grads/pallas_call | solution.py:265
  (21 shorter events, 0.2 us)
Async XLA Ops:
  0.6 1.2 %copy-start = (bf16[128,2560]{1,0:T(8,128)(2,1)S(1)}, bf16[128,2560]{1,0:T(8,128)(2,1)}, u32[]{:S(2)}) copy-start(bf16[128,2560]{1,0:T(8,128)(2,1)} %o_ref.5) | copy-start | bytes 1966084
  1.8 1.1 %copy-start.1 = (bf16[128,2560]{1,0:T(8,128)(2,1)S(1)}, bf16[128,2560]{1,0:T(8,128)(2,1)}, u32[]{:S(2)}) copy-start(bf16[128,2560]{1,0:T(8,128)(2,1)} %q_ref.1) | copy-start | bytes 1966084
  2.1 1.1 %copy-start.4 = (bf16[1,20,16,128]{3,2,1,0:T(8,128)(2,1)S(1)}, bf16[1,20,16,128]{3,2,1,0:T(8,128)(2,1)}, u32[]{:S(2)}) copy-start(bf16[1,20,16,128]{3,2,1,0:T(8,128)(2,1)} %param.9) | copy-start | bytes 245764
  2.1 4.1 %collective-permute-start.1 = (bf16[1280,128]{1,0:T(8,128)(2,1)S(1)}, bf16[1280,128]{1,0:T(8,128)(2,1)S(1)}, u32[]{:S(2)}, u32[]{:S(2)}) collective-permute-start(bf16[1280,128]{1,0:T(8,128)(2,1)S(1)} %partial_other.1), channel_id=1, source_target_pairs={{0,1},{1,0},{2,3},{3,2},{4,5},{5,4},{6,7},{7,6},{8,9},{9,8},{10,11... | collective-permute-start | bytes 983048 | tf_op jit(solution)/shard_map/ppermute | solution.py:50
  3.2 6.6 %collective-permute-start = (bf16[1,20,16,128]{3,2,1,0:T(8,128)(2,1)S(1)}, bf16[1,20,16,128]{3,2,1,0:T(8,128)(2,1)S(1)}, u32[]{:S(2)}, u32[]{:S(2)}) collective-permute-start(bf16[1,20,16,128]{3,2,1,0:T(8,128)(2,1)S(1)} %copy-done.4), channel_id=1, source_target_pairs={{0,2},{1,3},{2,0},{3,1},{4,6},{5,7},{6,4},{7,5},{8,10},{9,11},{10,... | collective-permute-start | bytes 245768 | tf_op jit(solution)/shard_map/ppermute | solution.py:59
  6.3 5.9 %collective-permute-start.2 = (bf16[320,128]{1,0:T(8,128)(2,1)S(1)}, bf16[320,128]{1,0:T(8,128)(2,1)S(1)}, u32[]{:S(2)}, u32[]{:S(2)}) collective-permute-start(bf16[320,128]{1,0:T(8,128)(2,1)S(1)} %get-tuple-element.16), channel_id=1, source_target_pairs={{0,6},{1,7},{2,4},{3,5},{4,2},{5,3},{6,0},{7,1},{8,14},{9,15},{10,... | collective-permute-start | bytes 245768 | tf_op jit(solution)/shard_map/ppermute | solution.py:59
  7.8 5.5 %collective-permute-start.3 = (bf16[320,128]{1,0:T(8,128)(2,1)S(1)}, bf16[320,128]{1,0:T(8,128)(2,1)S(1)}, u32[]{:S(2)}, u32[]{:S(2)}) collective-permute-start(bf16[320,128]{1,0:T(8,128)(2,1)S(1)} %get-tuple-element.17), channel_id=1, source_target_pairs={{0,4},{1,5},{2,6},{3,7},{4,0},{5,1},{6,2},{7,3},{8,12},{9,13},{10,... | collective-permute-start | bytes 245768 | tf_op jit(solution)/shard_map/ppermute | solution.py:59
  8.3 5.0 %collective-permute-start.4 = (bf16[320,128]{1,0:T(8,128)(2,1)S(1)}, bf16[320,128]{1,0:T(8,128)(2,1)S(1)}, u32[]{:S(2)}, u32[]{:S(2)}) collective-permute-start(bf16[320,128]{1,0:T(8,128)(2,1)S(1)} %get-tuple-element.18), channel_id=1, source_target_pairs={{0,2},{1,3},{2,0},{3,1},{4,6},{5,7},{6,4},{7,5},{8,10},{9,11},{10,... | collective-permute-start | bytes 245768 | tf_op jit(solution)/shard_map/ppermute | solution.py:59
  13.4 4.5 %collective-permute-start.7 = (bf16[320,128]{1,0:T(8,128)(2,1)S(1)}, bf16[320,128]{1,0:T(8,128)(2,1)S(1)}, u32[]{:S(2)}, u32[]{:S(2)}) collective-permute-start(bf16[320,128]{1,0:T(8,128)(2,1)S(1)} %get-tuple-element.23), channel_id=1, source_target_pairs={{0,8},{8,0},{16,24},{24,16},{1,9},{9,1},{17,25},{25,17},{2,10},{10... | collective-permute-start | bytes 245768 | tf_op jit(solution)/shard_map/ppermute | solution.py:294
  15.1 15.2 %copy-start.2 = (bf16[128,2560]{1,0:T(8,128)(2,1)S(1)}, bf16[128,2560]{1,0:T(8,128)(2,1)}, u32[]{:S(2)}) copy-start(bf16[128,2560]{1,0:T(8,128)(2,1)} %k_ref.3) | copy-start | bytes 1966084
  15.1 15.2 %copy-start.3 = (bf16[128,2560]{1,0:T(8,128)(2,1)S(1)}, bf16[128,2560]{1,0:T(8,128)(2,1)}, u32[]{:S(2)}) copy-start(bf16[128,2560]{1,0:T(8,128)(2,1)} %v_ref.3) | copy-start | bytes 1966084
  15.1 5.6 %collective-permute-start.5 = (bf16[2,20,16,128]{3,2,1,0:T(8,128)(2,1)S(1)}, bf16[2,20,16,128]{3,2,1,0:T(8,128)(2,1)S(1)}, u32[]{:S(2)}, u32[]{:S(2)}) collective-permute-start(bf16[2,20,16,128]{3,2,1,0:T(8,128)(2,1)S(1)} %pad_maximum_fusion.1), channel_id=1, source_target_pairs={{0,4},{1,5},{2,6},{3,7},{4,0},{5,1},{6,2},{7,3},{8,12},{9,13},{10,... | collective-permute-start | bytes 491528 | tf_op jit(solution)/shard_map/ppermute | solution.py:59
  17.9 5.4 %collective-permute-start.8 = (bf16[320,128]{1,0:T(8,128)(2,1)S(1)}, bf16[320,128]{1,0:T(8,128)(2,1)S(1)}, u32[]{:S(2)}, u32[]{:S(2)}) collective-permute-start(bf16[320,128]{1,0:T(8,128)(2,1)S(1)} %fusion.3), channel_id=1, source_target_pairs={{0,16},{8,24},{16,0},{24,8},{1,17},{9,25},{17,1},{25,9},{2,18},{10... | collective-permute-start | bytes 245768 | tf_op jit(solution)/shard_map/ppermute | solution.py:294
  20.7 9.5 %collective-permute-start.6 = (bf16[4,20,16,128]{3,2,1,0:T(8,128)(2,1)S(1)}, bf16[4,20,16,128]{3,2,1,0:T(8,128)(2,1)S(1)}, u32[]{:S(2)}, u32[]{:S(2)}) collective-permute-start(bf16[4,20,16,128]{3,2,1,0:T(8,128)(2,1)S(1)} %pad_maximum_fusion.rest_0_), channel_id=1, source_target_pairs={{0,1},{1,0},{2,3},{3,2},{4,5},{5,4},{6,7},{7,6},{8,9},{9,8},{10,11... | collective-permute-start | bytes 983048 | tf_op jit(solution)/shard_map/ppermute | solution.py:50
  23.4 5.4 %collective-permute-start.11 = (bf16[320,128]{1,0:T(8,128)(2,1)S(1)}, bf16[320,128]{1,0:T(8,128)(2,1)S(1)}, u32[]{:S(2)}, u32[]{:S(2)}) collective-permute-start(bf16[320,128]{1,0:T(8,128)(2,1)S(1)} %fusion.2.rest_2_), channel_id=1, source_target_pairs={{0,6},{1,7},{2,4},{3,5},{4,2},{5,3},{6,0},{7,1},{8,14},{9,15},{10,... | collective-permute-start | bytes 245768 | tf_op jit(solution)/shard_map/ppermute | solution.py:59
  25.3 4.4 %collective-permute-start.10 = (bf16[320,128]{1,0:T(8,128)(2,1)S(1)}, bf16[320,128]{1,0:T(8,128)(2,1)S(1)}, u32[]{:S(2)}, u32[]{:S(2)}) collective-permute-start(bf16[320,128]{1,0:T(8,128)(2,1)S(1)} %fusion.2.rest_2_), channel_id=1, source_target_pairs={{0,4},{1,5},{2,6},{3,7},{4,0},{5,1},{6,2},{7,3},{8,12},{9,13},{10,... | collective-permute-start | bytes 245768 | tf_op jit(solution)/shard_map/ppermute | solution.py:59
  25.8 4.4 %collective-permute-start.9 = (bf16[320,128]{1,0:T(8,128)(2,1)S(1)}, bf16[320,128]{1,0:T(8,128)(2,1)S(1)}, u32[]{:S(2)}, u32[]{:S(2)}) collective-permute-start(bf16[320,128]{1,0:T(8,128)(2,1)S(1)} %fusion.2.rest_2_), channel_id=1, source_target_pairs={{0,2},{1,3},{2,0},{3,1},{4,6},{5,7},{6,4},{7,5},{8,10},{9,11},{10,... | collective-permute-start | bytes 245768 | tf_op jit(solution)/shard_map/ppermute | solution.py:59
  26.9 4.4 %collective-permute-start.12 = (bf16[320,128]{1,0:T(8,128)(2,1)S(1)}, bf16[320,128]{1,0:T(8,128)(2,1)S(1)}, u32[]{:S(2)}, u32[]{:S(2)}) collective-permute-start(bf16[320,128]{1,0:T(8,128)(2,1)S(1)} %fusion.2.rest_2_), channel_id=1, source_target_pairs={{0,1},{1,0},{2,3},{3,2},{4,5},{5,4},{6,7},{7,6},{8,9},{9,8},{10,11... | collective-permute-start | bytes 245768 | tf_op jit(solution)/shard_map/ppermute | solution.py:50
  28.8 2.5 %collective-permute-start.15 = (bf16[320,128]{1,0:T(8,128)(2,1)S(1)}, bf16[320,128]{1,0:T(8,128)(2,1)S(1)}, u32[]{:S(2)}, u32[]{:S(2)}) collective-permute-start(bf16[320,128]{1,0:T(8,128)(2,1)S(1)} %collective-permute-done.11.rest_5_), channel_id=1, source_target_pairs={{0,1},{1,0},{2,3},{3,2},{4,5},{5,4},{6,7},{7,6},{8,9},{9,8},{10,11... | collective-permute-start | bytes 245768 | tf_op jit(solution)/shard_map/ppermute | solution.py:50
  29.8 1.6 %collective-permute-start.14 = (bf16[320,128]{1,0:T(8,128)(2,1)S(1)}, bf16[320,128]{1,0:T(8,128)(2,1)S(1)}, u32[]{:S(2)}, u32[]{:S(2)}) collective-permute-start(bf16[320,128]{1,0:T(8,128)(2,1)S(1)} %collective-permute-done.10.rest_4_), channel_id=1, source_target_pairs={{0,1},{1,0},{2,3},{3,2},{4,5},{5,4},{6,7},{7,6},{8,9},{9,8},{10,11... | collective-permute-start | bytes 245768 | tf_op jit(solution)/shard_map/ppermute | solution.py:50
  30.3 1.3 %collective-permute-start.13 = (bf16[320,128]{1,0:T(8,128)(2,1)S(1)}, bf16[320,128]{1,0:T(8,128)(2,1)S(1)}, u32[]{:S(2)}, u32[]{:S(2)}) collective-permute-start(bf16[320,128]{1,0:T(8,128)(2,1)S(1)} %collective-permute-done.9.rest_3_), channel_id=1, source_target_pairs={{0,1},{1,0},{2,3},{3,2},{4,5},{5,4},{6,7},{7,6},{8,9},{9,8},{10,11... | collective-permute-start | bytes 245768 | tf_op jit(solution)/shard_map/ppermute | solution.py:50
where the time goes:
time: 33.2 us; the launch traced here: 33 us
  starting transfers between devices  16 us (48%)
  waiting for transfers between devices  11.5 us (35%)
  Pallas kernels  3.09 us (9%)
  local copies, waits for them, and re-layouts  1.45 us (4%)
  between operations  0.77 us (2%)
    ppermute x8, starting transfers between devices, hop_groups(): return lax.ppermute(value, 'space', pairs)  11.1 us
    ppermute x8, waiting for transfers between devices, hop_groups(): return lax.ppermute(value, 'space', pairs)  6.96 us
    ppermute x2, waiting for transfers between devices, suffix_sum(): lax.ppermute(total.astype(jnp.bfloat16), 'tm', pairs).astype(jnp.float32)  4.31 us
    ppermute x2, starting transfers between devices, suffix_sum(): lax.ppermute(total.astype(jnp.bfloat16), 'tm', pairs).astype(jnp.float32)  4.29 us
    pallas_call x1, Pallas kernels, far_grads(): pl.pallas_call(functools.partial(far_kernel, lanes, groups), out_shape=(j...  1.46 us
    dynamic_slice x1, local copies, waits for them, and re-layouts, per_device(): lax.dynamic_slice(queries, starts, (queries.shape[0], span), allow_negati...  1.06 us
    pallas_call x1, Pallas kernels, near_grads(): pl.pallas_call(functools.partial(near_kernel, lanes, groups), out_shape=(...  1.01 us
  transfers between devices with their start and end apart: 16, of which 9 were waited for; matrix products, arithmetic and copies ran while one was open for 0% of the time, Pallas kernels for 4%

commit v1 on v0

--- a/solution.py
+++ b/solution.py
@@ -224,11 +224,15 @@
 def far_kernel(lanes, groups, k_ref, v_ref, *rest):
     dq_ref, near, pieces = rest[0], rest[1:3], rest[3:-8]
     dq_hbm, *outs = rest[-8:-5]
-    state, dk_buf, dv_buf, sems, dq_sem = rest[-5:]
+    state, dk_buf, dv_buf, sems, dq_sems = rest[-5:]
     span, head = state.shape
     group, lane = place_on_space(lanes)
-    copies = [pltpu.make_async_copy(dq_ref, dq_hbm, dq_sem)]
-    copies[0].start()
+    copies = []
+    rows = dq_ref.shape[0] // dq_sems.shape[0]
+    for at in range(dq_sems.shape[0]):
+        mine = pl.ds(at * rows, rows)
+        copies.append(pltpu.make_async_copy(dq_ref.at[mine, :], dq_hbm.at[mine, :], dq_sems.at[at]))
+        copies[-1].start()
     for at in range(2):
         mine = pl.ds(pl.multiple_of(lane * span, head), span)
         copies.append(pltpu.make_async_copy(near[at], outs[at].at[:, mine], sems.at[at, 0]))
@@ -276,7 +280,7 @@
             pltpu.VMEM((tokens, span), keys.dtype),
             pltpu.VMEM((tokens, span), values.dtype),
             pltpu.SemaphoreType.DMA((2, 1 + math.gcd(span // head, 5))),
-            pltpu.SemaphoreType.DMA,
+            pltpu.SemaphoreType.DMA((math.gcd(tokens // 16, 4) if tokens % 16 == 0 else 1,)),
         ],
         compiler_params=pltpu.CompilerParams(vmem_limit_bytes=VMEM_BYTES),
         cost_estimate=cost(4 * tokens * span * head, *near),

time: 33.2 us -> 33.2 us (level)
  no operation moved by 1% of the time
where the time goes in v1:
time: 33.2 us; the launch traced here: 33 us
  starting transfers between devices  16 us (48%)
  waiting for transfers between devices  11.5 us (35%)
  Pallas kernels  3.12 us (9%)
  local copies, waits for them, and re-layouts  1.45 us (4%)
  between operations  0.77 us (2%)
    ppermute x8, starting transfers between devices, hop_groups(): return lax.ppermute(value, 'space', pairs)  11.1 us
    ppermute x8, waiting for transfers between devices, hop_groups(): return lax.ppermute(value, 'space', pairs)  6.96 us
    ppermute x2, waiting for transfers between devices, suffix_sum(): lax.ppermute(total.astype(jnp.bfloat16), 'tm', pairs).astype(jnp.float32)  4.31 us
    ppermute x2, starting transfers between devices, suffix_sum(): lax.ppermute(total.astype(jnp.bfloat16), 'tm', pairs).astype(jnp.float32)  4.29 us
    pallas_call x1, Pallas kernels, far_grads(): pl.pallas_call(functools.partial(far_kernel, lanes, groups), out_shape=(j...  1.48 us
    dynamic_slice x1, local copies, waits for them, and re-layouts, per_device(): lax.dynamic_slice(queries, starts, (queries.shape[0], span), allow_negati...  1.06 us
    pallas_call x1, Pallas kernels, near_grads(): pl.pallas_call(functools.partial(near_kernel, lanes, groups), out_shape=(...  1.01 us
  transfers between devices with their start and end apart: 16, of which 9 were waited for; matrix products, arithmetic and copies ran while one was open for 0% of the time, Pallas kernels for 4%

profile of v1, /device:TPU:0, one launch (start us, length us, event | category | flops | bytes accessed | tf_op | source)
XLA Modules:
  0.0 33.0 jit_solution(5937360955217178609)
XLA Ops:
  0.6 1.1 %constant_dynamic-slice_fusion.q_ref = bf16[128,1280]{1,0:T(8,128)(2,1)S(1)} fusion(bf16[128,2560]{1,0:T(8,128)(2,1)} %q_ref.1, s32[]{:T(128)S(6)} %mul.3), kind=kLoop, calls=%fused_computation.9 | loop fusion | bytes 655364 | tf_op jit(solution)/shard_map/dynamic_slice | solution.py:324
  1.7 0.1 copy-done
  1.8 0.3 partial_other.1
  2.1 0.0 copy-start.4
  2.1 0.5 %collective-permute-start.1 = (bf16[1280,128]{1,0:T(8,128)(2,1)S(1)}, bf16[1280,128]{1,0:T(8,128)(2,1)S(1)}, u32[]{:S(2)}, u32[]{:S(2)}) collective-permute-start(bf16[1280,128]{1,0:T(8,128)(2,1)S(1)} %partial_other.1), channel_id=1, source_target_pairs={{0,1},{1,0},{2,3},{3,2},{4,5},{5,4},{6,7},{7,6},{8,9},{9,8},{10,11... | collective-permute-start | bytes 983048 | tf_op jit(solution)/shard_map/ppermute | solution.py:50
  2.6 0.3 copy-done.1
  2.9 0.3 partial_own.1.refs_0_
  3.2 3.0 %collective-permute-start = (bf16[1,20,16,128]{3,2,1,0:T(8,128)(2,1)S(1)}, bf16[1,20,16,128]{3,2,1,0:T(8,128)(2,1)S(1)}, u32[]{:S(2)}, u32[]{:S(2)}) collective-permute-start(bf16[1,20,16,128]{3,2,1,0:T(8,128)(2,1)S(1)} %copy-done.4), channel_id=1, source_target_pairs={{0,2},{1,3},{2,0},{3,1},{4,6},{5,7},{6,4},{7,5},{8,10},{9,11},{10,... | collective-permute-start | bytes 245768 | tf_op jit(solution)/shard_map/ppermute | solution.py:59
  6.2 0.1 cut_by_group.1
  6.3 1.6 %collective-permute-start.2 = (bf16[320,128]{1,0:T(8,128)(2,1)S(1)}, bf16[320,128]{1,0:T(8,128)(2,1)S(1)}, u32[]{:S(2)}, u32[]{:S(2)}) collective-permute-start(bf16[320,128]{1,0:T(8,128)(2,1)S(1)} %get-tuple-element.16), channel_id=1, source_target_pairs={{0,6},{1,7},{2,4},{3,5},{4,2},{5,3},{6,0},{7,1},{8,14},{9,15},{10,... | collective-permute-start | bytes 245768 | tf_op jit(solution)/shard_map/ppermute | solution.py:59
  7.8 0.5 %collective-permute-start.3 = (bf16[320,128]{1,0:T(8,128)(2,1)S(1)}, bf16[320,128]{1,0:T(8,128)(2,1)S(1)}, u32[]{:S(2)}, u32[]{:S(2)}) collective-permute-start(bf16[320,128]{1,0:T(8,128)(2,1)S(1)} %get-tuple-element.17), channel_id=1, source_target_pairs={{0,4},{1,5},{2,6},{3,7},{4,0},{5,1},{6,2},{7,3},{8,12},{9,13},{10,... | collective-permute-start | bytes 245768 | tf_op jit(solution)/shard_map/ppermute | solution.py:59
  8.3 1.5 %collective-permute-start.4 = (bf16[320,128]{1,0:T(8,128)(2,1)S(1)}, bf16[320,128]{1,0:T(8,128)(2,1)S(1)}, u32[]{:S(2)}, u32[]{:S(2)}) collective-permute-start(bf16[320,128]{1,0:T(8,128)(2,1)S(1)} %get-tuple-element.18), channel_id=1, source_target_pairs={{0,2},{1,3},{2,0},{3,1},{4,6},{5,7},{6,4},{7,5},{8,10},{9,11},{10,... | collective-permute-start | bytes 245768 | tf_op jit(solution)/shard_map/ppermute | solution.py:59
  9.8 2.4 %collective-permute-done.2 = bf16[320,128]{1,0:T(8,128)(2,1)S(1)} collective-permute-done((bf16[320,128]{1,0:T(8,128)(2,1)S(1)}, bf16[320,128]{1,0:T(8,128)(2,1)S(1)}, u32[]{:S(2)}, u32[]{:S(2)}) %collective-permute-start.2) | collective-permute-done | bytes 81952 | tf_op jit(solution)/shard_map/ppermute | solution.py:59
  12.2 1.2 %collective-permute-done.3 = bf16[320,128]{1,0:T(8,128)(2,1)S(1)} collective-permute-done((bf16[320,128]{1,0:T(8,128)(2,1)S(1)}, bf16[320,128]{1,0:T(8,128)(2,1)S(1)}, u32[]{:S(2)}, u32[]{:S(2)}) %collective-permute-start.3) | collective-permute-done | bytes 81952 | tf_op jit(solution)/shard_map/ppermute | solution.py:59
  13.4 1.6 %collective-permute-start.7 = (bf16[320,128]{1,0:T(8,128)(2,1)S(1)}, bf16[320,128]{1,0:T(8,128)(2,1)S(1)}, u32[]{:S(2)}, u32[]{:S(2)}) collective-permute-start(bf16[320,128]{1,0:T(8,128)(2,1)S(1)} %get-tuple-element.23), channel_id=1, source_target_pairs={{0,8},{8,0},{16,24},{24,16},{1,9},{9,1},{17,25},{25,17},{2,10},{10... | collective-permute-start | bytes 245768 | tf_op jit(solution)/shard_map/ppermute | solution.py:298
  15.1 0.0 copy-start.2
  15.1 1.0 %collective-permute-start.5 = (bf16[2,20,16,128]{3,2,1,0:T(8,128)(2,1)S(1)}, bf16[2,20,16,128]{3,2,1,0:T(8,128)(2,1)S(1)}, u32[]{:S(2)}, u32[]{:S(2)}) collective-permute-start(bf16[2,20,16,128]{3,2,1,0:T(8,128)(2,1)S(1)} %pad_maximum_fusion.1), channel_id=1, source_target_pairs={{0,4},{1,5},{2,6},{3,7},{4,0},{5,1},{6,2},{7,3},{8,12},{9,13},{10,... | collective-permute-start | bytes 491528 | tf_op jit(solution)/shard_map/ppermute | solution.py:59
  16.1 1.8 %collective-permute-done.7 = bf16[320,128]{1,0:T(8,128)(2,1)S(1)} collective-permute-done((bf16[320,128]{1,0:T(8,128)(2,1)S(1)}, bf16[320,128]{1,0:T(8,128)(2,1)S(1)}, u32[]{:S(2)}, u32[]{:S(2)}) %collective-permute-start.7) | collective-permute-done | bytes 81952 | tf_op jit(solution)/shard_map/ppermute | solution.py:298
  17.9 2.7 %collective-permute-start.8 = (bf16[320,128]{1,0:T(8,128)(2,1)S(1)}, bf16[320,128]{1,0:T(8,128)(2,1)S(1)}, u32[]{:S(2)}, u32[]{:S(2)}) collective-permute-start(bf16[320,128]{1,0:T(8,128)(2,1)S(1)} %fusion.3), channel_id=1, source_target_pairs={{0,16},{8,24},{16,0},{24,8},{1,17},{9,25},{17,1},{25,9},{2,18},{10... | collective-permute-start | bytes 245768 | tf_op jit(solution)/shard_map/ppermute | solution.py:298
  20.6 0.1 collective-permute-done.5
  20.7 0.1 collective-permute-start.6
  20.8 2.5 %collective-permute-done.8 = bf16[320,128]{1,0:T(8,128)(2,1)S(1)} collective-permute-done((bf16[320,128]{1,0:T(8,128)(2,1)S(1)}, bf16[320,128]{1,0:T(8,128)(2,1)S(1)}, u32[]{:S(2)}, u32[]{:S(2)}) %collective-permute-start.8) | collective-permute-done | bytes 81952 | tf_op jit(solution)/shard_map/ppermute | solution.py:298
  23.4 1.9 %collective-permute-start.11 = (bf16[320,128]{1,0:T(8,128)(2,1)S(1)}, bf16[320,128]{1,0:T(8,128)(2,1)S(1)}, u32[]{:S(2)}, u32[]{:S(2)}) collective-permute-start(bf16[320,128]{1,0:T(8,128)(2,1)S(1)} %fusion.2.rest_2_), channel_id=1, source_target_pairs={{0,6},{1,7},{2,4},{3,5},{4,2},{5,3},{6,0},{7,1},{8,14},{9,15},{10,... | collective-permute-start | bytes 245768 | tf_op jit(solution)/shard_map/ppermute | solution.py:59
  25.3 0.5 %collective-permute-start.10 = (bf16[320,128]{1,0:T(8,128)(2,1)S(1)}, bf16[320,128]{1,0:T(8,128)(2,1)S(1)}, u32[]{:S(2)}, u32[]{:S(2)}) collective-permute-start(bf16[320,128]{1,0:T(8,128)(2,1)S(1)} %fusion.2.rest_2_), channel_id=1, source_target_pairs={{0,4},{1,5},{2,6},{3,7},{4,0},{5,1},{6,2},{7,3},{8,12},{9,13},{10,... | collective-permute-start | bytes 245768 | tf_op jit(solution)/shard_map/ppermute | solution.py:59
  25.8 1.1 %collective-permute-start.9 = (bf16[320,128]{1,0:T(8,128)(2,1)S(1)}, bf16[320,128]{1,0:T(8,128)(2,1)S(1)}, u32[]{:S(2)}, u32[]{:S(2)}) collective-permute-start(bf16[320,128]{1,0:T(8,128)(2,1)S(1)} %fusion.2.rest_2_), channel_id=1, source_target_pairs={{0,2},{1,3},{2,0},{3,1},{4,6},{5,7},{6,4},{7,5},{8,10},{9,11},{10,... | collective-permute-start | bytes 245768 | tf_op jit(solution)/shard_map/ppermute | solution.py:59
  26.9 1.8 %collective-permute-done.11.rest_5_ = bf16[320,128]{1,0:T(8,128)(2,1)S(1)} collective-permute-done((bf16[320,128]{1,0:T(8,128)(2,1)S(1)}, bf16[320,128]{1,0:T(8,128)(2,1)S(1)}, u32[]{:S(2)}, u32[]{:S(2)}) %collective-permute-start.11) | collective-permute-done | bytes 81952 | tf_op jit(solution)/shard_map/ppermute | solution.py:59
  28.8 1.0 %collective-permute-done.10.rest_4_ = bf16[320,128]{1,0:T(8,128)(2,1)S(1)} collective-permute-done((bf16[320,128]{1,0:T(8,128)(2,1)S(1)}, bf16[320,128]{1,0:T(8,128)(2,1)S(1)}, u32[]{:S(2)}, u32[]{:S(2)}) %collective-permute-start.10) | collective-permute-done | bytes 81952 | tf_op jit(solution)/shard_map/ppermute | solution.py:59
  29.8 0.5 %collective-permute-done.9.rest_3_ = bf16[320,128]{1,0:T(8,128)(2,1)S(1)} collective-permute-done((bf16[320,128]{1,0:T(8,128)(2,1)S(1)}, bf16[320,128]{1,0:T(8,128)(2,1)S(1)}, u32[]{:S(2)}, u32[]{:S(2)}) %collective-permute-start.9) | collective-permute-done | bytes 81952 | tf_op jit(solution)/shard_map/ppermute | solution.py:59
  30.3 0.0 collective-permute-start.13
  30.3 1.0 %near_grads.1 = (bf16[128,2560]{1,0:T(8,128)(2,1)S(1)}, bf16[128,1280]{1,0:T(8,128)(2,1)S(1)}, bf16[128,1280]{1,0:T(8,128)(2,1)S(1)}) custom-call(bf16[128,2560]{1,0:T(8,128)(2,1)S(1)} %copy-done.1, bf16[128,2560]{1,0:T(8,128)(2,1)S(1)} %copy-done, bf16[128,2560]{1,0:T(8,128)(2,1)S(1)} %copy-done.2, bf16[128,2560]{1,0:T(8,128)(2,1)S(1)} %copy-done.3, ...), custom_call_target="tpu_custom_call" | custom-call | flops 167772160 | bytes 2621440 | tf_op jit(solution)/shard_map/near_grads/pallas_call | solution.py:204
  31.3 0.2 collective-permute-done.13.rest_4_
  31.5 1.5 %far_grads.1 = (bf16[128,2560]{1,0:T(8,128)(2,1)}, bf16[128,2560]{1,0:T(8,128)(2,1)}, bf16[128,2560]{1,0:T(8,128)(2,1)}) custom-call(bf16[128,2560]{1,0:T(8,128)(2,1)S(1)} %copy-done.2, bf16[128,2560]{1,0:T(8,128)(2,1)S(1)} %copy-done.3, bf16[128,2560]{1,0:T(8,128)(2,1)S(1)} %get-tuple-element.20.rest_0_, bf16[128,1280]{1,0:T(8,128)(2,1)S(1)} %get-tuple-element.21.rest_1_, ...), custom_call_target="tpu_custom_call" | custom-call | flops 83886080 | bytes 1310720 | tf_op jit(solution)/shard_map/far_grads/pallas_call | solution.py:269
  (21 shorter events, 0.2 us)
Async XLA Ops:
  0.6 1.2 %copy-start = (bf16[128,2560]{1,0:T(8,128)(2,1)S(1)}, bf16[128,2560]{1,0:T(8,128)(2,1)}, u32[]{:S(2)}) copy-start(bf16[128,2560]{1,0:T(8,128)(2,1)} %o_ref.5) | copy-start | bytes 1966084
  1.8 1.1 %copy-start.1 = (bf16[128,2560]{1,0:T(8,128)(2,1)S(1)}, bf16[128,2560]{1,0:T(8,128)(2,1)}, u32[]{:S(2)}) copy-start(bf16[128,2560]{1,0:T(8,128)(2,1)} %q_ref.1) | copy-start | bytes 1966084
  2.1 1.1 %copy-start.4 = (bf16[1,20,16,128]{3,2,1,0:T(8,128)(2,1)S(1)}, bf16[1,20,16,128]{3,2,1,0:T(8,128)(2,1)}, u32[]{:S(2)}) copy-start(bf16[1,20,16,128]{3,2,1,0:T(8,128)(2,1)} %param.9) | copy-start | bytes 245764
  2.1 4.1 %collective-permute-start.1 = (bf16[1280,128]{1,0:T(8,128)(2,1)S(1)}, bf16[1280,128]{1,0:T(8,128)(2,1)S(1)}, u32[]{:S(2)}, u32[]{:S(2)}) collective-permute-start(bf16[1280,128]{1,0:T(8,128)(2,1)S(1)} %partial_other.1), channel_id=1, source_target_pairs={{0,1},{1,0},{2,3},{3,2},{4,5},{5,4},{6,7},{7,6},{8,9},{9,8},{10,11... | collective-permute-start | bytes 983048 | tf_op jit(solution)/shard_map/ppermute | solution.py:50
  3.2 6.6 %collective-permute-start = (bf16[1,20,16,128]{3,2,1,0:T(8,128)(2,1)S(1)}, bf16[1,20,16,128]{3,2,1,0:T(8,128)(2,1)S(1)}, u32[]{:S(2)}, u32[]{:S(2)}) collective-permute-start(bf16[1,20,16,128]{3,2,1,0:T(8,128)(2,1)S(1)} %copy-done.4), channel_id=1, source_target_pairs={{0,2},{1,3},{2,0},{3,1},{4,6},{5,7},{6,4},{7,5},{8,10},{9,11},{10,... | collective-permute-start | bytes 245768 | tf_op jit(solution)/shard_map/ppermute | solution.py:59
  6.3 5.9 %collective-permute-start.2 = (bf16[320,128]{1,0:T(8,128)(2,1)S(1)}, bf16[320,128]{1,0:T(8,128)(2,1)S(1)}, u32[]{:S(2)}, u32[]{:S(2)}) collective-permute-start(bf16[320,128]{1,0:T(8,128)(2,1)S(1)} %get-tuple-element.16), channel_id=1, source_target_pairs={{0,6},{1,7},{2,4},{3,5},{4,2},{5,3},{6,0},{7,1},{8,14},{9,15},{10,... | collective-permute-start | bytes 245768 | tf_op jit(solution)/shard_map/ppermute | solution.py:59
  7.8 5.5 %collective-permute-start.3 = (bf16[320,128]{1,0:T(8,128)(2,1)S(1)}, bf16[320,128]{1,0:T(8,128)(2,1)S(1)}, u32[]{:S(2)}, u32[]{:S(2)}) collective-permute-start(bf16[320,128]{1,0:T(8,128)(2,1)S(1)} %get-tuple-element.17), channel_id=1, source_target_pairs={{0,4},{1,5},{2,6},{3,7},{4,0},{5,1},{6,2},{7,3},{8,12},{9,13},{10,... | collective-permute-start | bytes 245768 | tf_op jit(solution)/shard_map/ppermute | solution.py:59
  8.3 5.0 %collective-permute-start.4 = (bf16[320,128]{1,0:T(8,128)(2,1)S(1)}, bf16[320,128]{1,0:T(8,128)(2,1)S(1)}, u32[]{:S(2)}, u32[]{:S(2)}) collective-permute-start(bf16[320,128]{1,0:T(8,128)(2,1)S(1)} %get-tuple-element.18), channel_id=1, source_target_pairs={{0,2},{1,3},{2,0},{3,1},{4,6},{5,7},{6,4},{7,5},{8,10},{9,11},{10,... | collective-permute-start | bytes 245768 | tf_op jit(solution)/shard_map/ppermute | solution.py:59
  13.4 4.5 %collective-permute-start.7 = (bf16[320,128]{1,0:T(8,128)(2,1)S(1)}, bf16[320,128]{1,0:T(8,128)(2,1)S(1)}, u32[]{:S(2)}, u32[]{:S(2)}) collective-permute-start(bf16[320,128]{1,0:T(8,128)(2,1)S(1)} %get-tuple-element.23), channel_id=1, source_target_pairs={{0,8},{8,0},{16,24},{24,16},{1,9},{9,1},{17,25},{25,17},{2,10},{10... | collective-permute-start | bytes 245768 | tf_op jit(solution)/shard_map/ppermute | solution.py:298
  15.1 15.2 %copy-start.2 = (bf16[128,2560]{1,0:T(8,128)(2,1)S(1)}, bf16[128,2560]{1,0:T(8,128)(2,1)}, u32[]{:S(2)}) copy-start(bf16[128,2560]{1,0:T(8,128)(2,1)} %k_ref.3) | copy-start | bytes 1966084
  15.1 15.2 %copy-start.3 = (bf16[128,2560]{1,0:T(8,128)(2,1)S(1)}, bf16[128,2560]{1,0:T(8,128)(2,1)}, u32[]{:S(2)}) copy-start(bf16[128,2560]{1,0:T(8,128)(2,1)} %v_ref.3) | copy-start | bytes 1966084
  15.1 5.6 %collective-permute-start.5 = (bf16[2,20,16,128]{3,2,1,0:T(8,128)(2,1)S(1)}, bf16[2,20,16,128]{3,2,1,0:T(8,128)(2,1)S(1)}, u32[]{:S(2)}, u32[]{:S(2)}) collective-permute-start(bf16[2,20,16,128]{3,2,1,0:T(8,128)(2,1)S(1)} %pad_maximum_fusion.1), channel_id=1, source_target_pairs={{0,4},{1,5},{2,6},{3,7},{4,0},{5,1},{6,2},{7,3},{8,12},{9,13},{10,... | collective-permute-start | bytes 491528 | tf_op jit(solution)/shard_map/ppermute | solution.py:59
  17.9 5.4 %collective-permute-start.8 = (bf16[320,128]{1,0:T(8,128)(2,1)S(1)}, bf16[320,128]{1,0:T(8,128)(2,1)S(1)}, u32[]{:S(2)}, u32[]{:S(2)}) collective-permute-start(bf16[320,128]{1,0:T(8,128)(2,1)S(1)} %fusion.3), channel_id=1, source_target_pairs={{0,16},{8,24},{16,0},{24,8},{1,17},{9,25},{17,1},{25,9},{2,18},{10... | collective-permute-start | bytes 245768 | tf_op jit(solution)/shard_map/ppermute | solution.py:298
  20.7 9.5 %collective-permute-start.6 = (bf16[4,20,16,128]{3,2,1,0:T(8,128)(2,1)S(1)}, bf16[4,20,16,128]{3,2,1,0:T(8,128)(2,1)S(1)}, u32[]{:S(2)}, u32[]{:S(2)}) collective-permute-start(bf16[4,20,16,128]{3,2,1,0:T(8,128)(2,1)S(1)} %pad_maximum_fusion.rest_0_), channel_id=1, source_target_pairs={{0,1},{1,0},{2,3},{3,2},{4,5},{5,4},{6,7},{7,6},{8,9},{9,8},{10,11... | collective-permute-start | bytes 983048 | tf_op jit(solution)/shard_map/ppermute | solution.py:50
  23.4 5.4 %collective-permute-start.11 = (bf16[320,128]{1,0:T(8,128)(2,1)S(1)}, bf16[320,128]{1,0:T(8,128)(2,1)S(1)}, u32[]{:S(2)}, u32[]{:S(2)}) collective-permute-start(bf16[320,128]{1,0:T(8,128)(2,1)S(1)} %fusion.2.rest_2_), channel_id=1, source_target_pairs={{0,6},{1,7},{2,4},{3,5},{4,2},{5,3},{6,0},{7,1},{8,14},{9,15},{10,... | collective-permute-start | bytes 245768 | tf_op jit(solution)/shard_map/ppermute | solution.py:59
  25.3 4.4 %collective-permute-start.10 = (bf16[320,128]{1,0:T(8,128)(2,1)S(1)}, bf16[320,128]{1,0:T(8,128)(2,1)S(1)}, u32[]{:S(2)}, u32[]{:S(2)}) collective-permute-start(bf16[320,128]{1,0:T(8,128)(2,1)S(1)} %fusion.2.rest_2_), channel_id=1, source_target_pairs={{0,4},{1,5},{2,6},{3,7},{4,0},{5,1},{6,2},{7,3},{8,12},{9,13},{10,... | collective-permute-start | bytes 245768 | tf_op jit(solution)/shard_map/ppermute | solution.py:59
  25.8 4.4 %collective-permute-start.9 = (bf16[320,128]{1,0:T(8,128)(2,1)S(1)}, bf16[320,128]{1,0:T(8,128)(2,1)S(1)}, u32[]{:S(2)}, u32[]{:S(2)}) collective-permute-start(bf16[320,128]{1,0:T(8,128)(2,1)S(1)} %fusion.2.rest_2_), channel_id=1, source_target_pairs={{0,2},{1,3},{2,0},{3,1},{4,6},{5,7},{6,4},{7,5},{8,10},{9,11},{10,... | collective-permute-start | bytes 245768 | tf_op jit(solution)/shard_map/ppermute | solution.py:59
  26.9 4.4 %collective-permute-start.12 = (bf16[320,128]{1,0:T(8,128)(2,1)S(1)}, bf16[320,128]{1,0:T(8,128)(2,1)S(1)}, u32[]{:S(2)}, u32[]{:S(2)}) collective-permute-start(bf16[320,128]{1,0:T(8,128)(2,1)S(1)} %fusion.2.rest_2_), channel_id=1, source_target_pairs={{0,1},{1,0},{2,3},{3,2},{4,5},{5,4},{6,7},{7,6},{8,9},{9,8},{10,11... | collective-permute-start | bytes 245768 | tf_op jit(solution)/shard_map/ppermute | solution.py:50
  28.8 2.5 %collective-permute-start.15 = (bf16[320,128]{1,0:T(8,128)(2,1)S(1)}, bf16[320,128]{1,0:T(8,128)(2,1)S(1)}, u32[]{:S(2)}, u32[]{:S(2)}) collective-permute-start(bf16[320,128]{1,0:T(8,128)(2,1)S(1)} %collective-permute-done.11.rest_5_), channel_id=1, source_target_pairs={{0,1},{1,0},{2,3},{3,2},{4,5},{5,4},{6,7},{7,6},{8,9},{9,8},{10,11... | collective-permute-start | bytes 245768 | tf_op jit(solution)/shard_map/ppermute | solution.py:50
  29.8 1.6 %collective-permute-start.14 = (bf16[320,128]{1,0:T(8,128)(2,1)S(1)}, bf16[320,128]{1,0:T(8,128)(2,1)S(1)}, u32[]{:S(2)}, u32[]{:S(2)}) collective-permute-start(bf16[320,128]{1,0:T(8,128)(2,1)S(1)} %collective-permute-done.10.rest_4_), channel_id=1, source_target_pairs={{0,1},{1,0},{2,3},{3,2},{4,5},{5,4},{6,7},{7,6},{8,9},{9,8},{10,11... | collective-permute-start | bytes 245768 | tf_op jit(solution)/shard_map/ppermute | solution.py:50
  30.3 1.3 %collective-permute-start.13 = (bf16[320,128]{1,0:T(8,128)(2,1)S(1)}, bf16[320,128]{1,0:T(8,128)(2,1)S(1)}, u32[]{:S(2)}, u32[]{:S(2)}) collective-permute-start(bf16[320,128]{1,0:T(8,128)(2,1)S(1)} %collective-permute-done.9.rest_3_), channel_id=1, source_target_pairs={{0,1},{1,0},{2,3},{3,2},{4,5},{5,4},{6,7},{7,6},{8,9},{9,8},{10,11... | collective-permute-start | bytes 245768 | tf_op jit(solution)/shard_map/ppermute | solution.py:50
